TPU v7x, 32 devices: a whole 2x2x4 slice. The times are simulated.
32 devices in a mesh: row: 4 (over y, x), col: 8 (over z, core).
Axes of the slice: x: 2, y: 2, z: 4, core: 2. Of those that a mesh axis runs over, the one named last changes fastest.
Arguments:
- local_tiles: bfloat16 [8192, 128, 128], P(('row', 'col')), may hold values from -0.109375 to 0.109375
- local_src: int32 [8192], P(('row', 'col')), may hold values from 0 to 15
- local_dst: int32 [8192], P(('row', 'col')), may hold values from 0 to 15
- local_count: int32 [32], P(('row', 'col')), may hold values from 128 to 256, as said below
- remote_tiles: bfloat16 [2048, 128, 128], P(('row', 'col')), may hold values from -0.109375 to 0.109375
- remote_src: int32 [2048], P(('row', 'col')), may hold values from 0 to 15
- remote_dst: int32 [2048], P(('row', 'col')), may hold values from 0 to 15
- bucket_count: int32 [32, 32], P(('row', 'col')), may hold values from 1 to 2, as said below
- hub_ids: int32 [256], P(('row', 'col')), may hold values from 0 to 65535, as said below
- hub_weights: bfloat16 [256, 65536], P(None, ('row', 'col')), may hold values from -0.109375 to 0.109375
- prior: float32 [65536, 128], P(('row', 'col')), may hold values from -6 to 6
- seed_ids: int32 [128], replicated, may hold values from 0 to 65535
Outputs:
- rank_vector: float32 [65536, 128], P(('row', 'col'))
- residual: float32 [65536, 128], P(('row', 'col'))
Inputs may be any that keep to these rules, and one draw needn't show every extreme that they name: `local_count`: each device has at least half of its 256 slots live; some device has all of them live. `bucket_count`: every bucket has at least one live slot; every device's bucket to some device is full, and some device receives full buckets from every device. `hub_ids`: the 8 entries of device i are distinct vertices of device i's own blocks.
All inputs are finite; a program needn't handle non-finite values.
Results may differ from a plain program's by a relative error of at most 0.009.
Values may be sent and summed in bfloat16 or wider, within the bound.
A program may use at most 128 MiB of HBM per device.

v0:
```python
import jax
import jax.numpy as jnp
from jax import lax
from jax.sharding import PartitionSpec as P

ITERS = 2


DAMPING = 0.85


def body(
    local_tiles,
    local_src,
    local_dst,
    local_count,
    remote_tiles,
    remote_src,
    remote_dst,
    bucket_count,
    hub_ids,
    hub_weights,
    prior,
    seed_ids,
):
    device_count = lax.axis_size(("row", "col"))
    own_index = lax.axis_index(("row", "col"))
    vertex_rows = prior.shape[0]
    seed_count = prior.shape[1]
    tile_size = local_tiles.shape[1]
    block_count = vertex_rows // tile_size
    slot_total = remote_src.shape[0]
    capacity = slot_total // device_count
    vertex_ids = own_index * vertex_rows + jnp.arange(vertex_rows, dtype=jnp.int32)
    teleport = prior + 4.0 * (vertex_ids[:, None] == seed_ids[None, :]).astype(jnp.float32)
    hub_local = hub_ids - own_index * vertex_rows
    non_hub = jnp.logical_not(
        jnp.any(jnp.arange(vertex_rows, dtype=jnp.int32)[:, None] == hub_local[None, :], axis=1)
    )
    local_live = (jnp.arange(local_src.shape[0], dtype=jnp.int32) < local_count[0]).astype(
        jnp.float32
    )
    local_select = (jnp.arange(block_count, dtype=jnp.int32)[:, None] == local_dst[None, :]).astype(
        jnp.float32
    ) * local_live[None, :]
    slot_index = jnp.arange(slot_total, dtype=jnp.int32)
    remote_live = (slot_index % capacity < bucket_count[0][slot_index // capacity]).astype(
        jnp.float32
    )
    targets = lax.all_to_all(
        remote_dst.reshape(device_count, capacity),
        ("row", "col"),
        split_axis=0,
        concat_axis=0,
        tiled=True,
    ).reshape(-1)
    remote_select = (jnp.arange(block_count, dtype=jnp.int32)[:, None] == targets[None, :]).astype(
        jnp.bfloat16
    )
    rank_vector = jnp.zeros((vertex_rows, seed_count), jnp.float32)
    residual = teleport
    for iteration in range(ITERS):
        sent_state = residual.astype(jnp.bfloat16)
        rank_vector = rank_vector + (1.0 - DAMPING) * residual
        masked = jnp.where(non_hub[:, None], sent_state, jnp.zeros_like(sent_state))
        own_blocks = masked.reshape(block_count, tile_size, seed_count)
        outgoing = (
            jnp.einsum(
                "tab,tas->tbs",
                remote_tiles,
                own_blocks[remote_src],
                preferred_element_type=jnp.float32,
            )
            * remote_live[:, None, None]
        ).astype(jnp.bfloat16)
        incoming = lax.all_to_all(
            outgoing.reshape(device_count, capacity, tile_size, seed_count),
            ("row", "col"),
            split_axis=0,
            concat_axis=0,
            tiled=True,
        )
        incoming = incoming.reshape(slot_total, tile_size * seed_count)
        local_products = jnp.einsum(
            "tab,tas->tbs", local_tiles, own_blocks[local_src], preferred_element_type=jnp.float32
        )
        local_terms = jnp.einsum("dt,tbs->dbs", local_select, local_products)
        remote_terms = jnp.dot(remote_select, incoming, preferred_element_type=jnp.float32)
        hub_state = sent_state[hub_local]
        group_hubs = lax.all_gather(hub_state, "col", axis=0, tiled=True)
        hub_terms = lax.dot_general(
            hub_weights,
            lax.all_gather(group_hubs, "row", axis=0, tiled=True),
            (((0,), (0,)), ((), ())),
            preferred_element_type=jnp.float32,
        )
        residual = DAMPING * (
            local_terms.reshape(vertex_rows, seed_count)
            + remote_terms.reshape(vertex_rows, seed_count)
            + hub_terms
        )
    return (rank_vector, residual)


def solution(mesh):
    placed = (
        P(("row", "col"), None, None),
        P(("row", "col")),
        P(("row", "col")),
        P(("row", "col")),
        P(("row", "col"), None, None),
        P(("row", "col")),
        P(("row", "col")),
        P(("row", "col"), None),
        P(("row", "col")),
        P(None, ("row", "col")),
        P(("row", "col"), None),
        P(),
    )
    return jax.shard_map(
        body,
        mesh=mesh,
        in_specs=placed,
        out_specs=(P(("row", "col"), None), P(("row", "col"), None)),
        check_vma=False,
    )
```

profile of v0, /device:TPU:0, one launch (start us, length us, event | category | flops | bytes accessed | tf_op | source)
XLA Modules:
  0.0 215.2 jit_solution(15108957775657509287)
XLA Ops:
  2.2 7.3 %all-to-all-start = ((s32[32,1,2]{2,1,0:T(1,128)}), s32[32,1,2]{2,1,0:T(1,128)S(1)}, u32[]{:S(2)}, u32[]{:S(2)}) async-start(s32[32,1,2]{2,1,0:T(1,128)} %bitcast.4), calls=%async_computation | async-start | bytes 32768 | tf_op jit(solution)/shard_map/all_to_all | solution.py:50
  18.1 4.0 %multiply_convert_fusion.1 = bf16[64,128,128]{2,1,0:T(8,128)(2,1)} fusion(bf16[64,128,128]{2,1,0:T(8,128)(2,1)} %gather_fusion.1, bf16[64,128,128]{2,1,0:T(8,128)(2,1)S(1)} %copy-done, f32[64]{0:T(128)S(1)} %compare_convert_fusion), kind=kOutput, calls=%fused_computation.12 | convolution fusion | flops 270532608 | bytes 6291712 | tf_op jit(solution)/shard_map/tab,tas->tbs/dot_general | solution.py:68
  22.1 4.1 %copy.70 = bf16[32,2,128,128]{3,2,1,0:T(8,128)(2,1)} copy(bf16[32,2,128,128]{2,3,1,0:T(8,128)(2,1)} %bitcast.70) | data formatting | bytes 4194304 | tf_op jit(solution)/shard_map/reshape | solution.py:77
  26.3 6.0 %all-to-all-start.1 = ((bf16[32,2,128,128]{3,2,1,0:T(8,128)(2,1)}), bf16[32,2,128,128]{3,2,1,0:T(8,128)(2,1)}, u32[]{:S(2)}, u32[]{:S(2)}) async-start(bf16[32,2,128,128]{3,2,1,0:T(8,128)(2,1)} %copy.70), calls=%async_computation.1 | async-start | bytes 4194304 | tf_op jit(solution)/shard_map/all_to_all | solution.py:76
  33.3 8.6 %gather_fusion = bf16[256,128,128]{2,1,0:T(8,128)(2,1)} fusion(bf16[16,128,128]{2,1,0:T(8,128)(2,1)S(1)} %bitcast.66, s32[1024]{0:T(1024)S(1)} %pad_clamp_fusion.3), kind=kCustom, calls=%fused_computation | custom fusion | bytes 16778240 | tf_op jit(solution)/shard_map/gather | solution.py:85
  41.9 9.4 %convolution_bitcast_fusion.1 = bf16[256,128,128]{1,2,0:T(8,128)(2,1)} fusion(bf16[256,128,128]{2,1,0:T(8,128)(2,1)} %gather_fusion, bf16[256,128,128]{2,1,0:T(8,128)(2,1)} %param.12), kind=kOutput, calls=%fused_computation.10 | convolution fusion | flops 1073741824 | bytes 25165824 | tf_op jit(solution)/shard_map/tab,tas->tbs/dot_general | solution.py:84
  51.3 12.2 %copy.65 = bf16[256,128,128]{2,0,1:T(8,128)(2,1)} copy(bf16[256,128,128]{1,2,0:T(8,128)(2,1)} %convolution_bitcast_fusion.1) | data formatting | bytes 16777216 | tf_op jit(solution)/shard_map/tab,tas->tbs/dot_general | solution.py:84
  64.1 4.6 %fusion.14 = f32[16,128,128]{2,0,1:T(8,128)S(1)} fusion(bf16[256,128,128]{2,0,1:T(8,128)(2,1)} %copy.65, bf16[256]{0:T(256)(128)(2,1)S(1)} %compare_convert_fusion.1, s32[256]{0:T(256)S(1)} %copy-done.6), kind=kOutput, calls=%fused_computation.34 | convolution fusion | flops 134225920 | bytes 9438720 | tf_op jit(solution)/shard_map/dt,tbs->dbs/dot_general | solution.py:87
  72.2 14.7 %all-gather = bf16[64,128]{1,0:T(8,128)(2,1)S(1)} all-gather(bf16[8,128]{1,0:T(8,128)(2,1)S(1)} %gather_fusion.3), channel_id=2, replica_groups=mesh['row'=4,'col'=8] {'col'}, dimensions={0}, use_global_device_ids=true | all-gather | bytes 18432 | tf_op jit(solution)/shard_map/all_gather | solution.py:90
  86.8 8.6 %all-gather.1 = bf16[256,128]{1,0:T(8,128)(2,1)S(1)} all-gather(bf16[64,128]{1,0:T(8,128)(2,1)S(1)} %all-gather), channel_id=3, replica_groups=mesh['row'=4,'col'=8] {'row'}, dimensions={0}, use_global_device_ids=true | all-gather | bytes 81920 | tf_op jit(solution)/shard_map/all_gather | solution.py:93
  96.7 3.8 %fusion.8 = f32[16,16384]{1,0:T(8,128)} fusion(bf16[8,8,128,128]{3,2,1,0:T(8,128)(2,1)} %bitcast.19, s32[64]{0:T(128)S(1)} %eq.66), kind=kOutput, calls=%fused_computation.21 | convolution fusion | flops 33555456 | bytes 3145984 | tf_op jit(solution)/shard_map/dot_general | solution.py:88
  102.9 2.5 %copy.72 = f32[2048,128]{0,1:T(8,128)} copy(f32[2048,128]{1,0:T(8,128)} %reshape.115) | data formatting | bytes 2097152 | tf_op jit(solution)/shard_map/reshape | solution.py:99
  105.5 3.3 %multiply_add_fusion = (f32[2048,128]{0,1:T(8,128)}, f32[2048,128]{0,1:T(8,128)S(1)}) fusion(f32[2048,128]{0,1:T(8,128)S(1)} %copy-done.3, s32[2048]{0:T(1024)S(1)} %iota_add_fusion, s32[128]{0:T(128)S(1)} %copy-done.7, bf16[256,128]{1,0:T(8,128)(2,1)S(1)} %all-gather.1, bf16[256,2048]{1,0:T(8,128)(2,1)} %param.21, f32[2048,128]{0,1:T(8,128)} %copy.71, ...), kind=kOutput, calls=%fused_computation.26 | convolution fusion | flops 136314880 | bytes 6365696 | tf_op jit(solution)/shard_map/dot_general | solution.py:91
  113.2 4.0 %multiply_convert_fusion = bf16[64,128,128]{2,1,0:T(8,128)(2,1)} fusion(bf16[64,128,128]{2,1,0:T(8,128)(2,1)} %gather_fusion.5, bf16[64,128,128]{2,1,0:T(8,128)(2,1)S(1)} %copy-done, f32[64]{0:T(128)S(1)} %compare_convert_fusion), kind=kOutput, calls=%fused_computation.11 | convolution fusion | flops 270532608 | bytes 6291712 | tf_op jit(solution)/shard_map/tab,tas->tbs/dot_general | solution.py:68
  117.3 4.1 %copy.80 = bf16[32,2,128,128]{3,2,1,0:T(8,128)(2,1)} copy(bf16[32,2,128,128]{2,3,1,0:T(8,128)(2,1)} %bitcast.69) | data formatting | bytes 4194304 | tf_op jit(solution)/shard_map/reshape | solution.py:77
  121.3 3.5 %all-to-all-start.2 = ((bf16[32,2,128,128]{3,2,1,0:T(8,128)(2,1)}), bf16[32,2,128,128]{3,2,1,0:T(8,128)(2,1)}, u32[]{:S(2)}, u32[]{:S(2)}) async-start(bf16[32,2,128,128]{3,2,1,0:T(8,128)(2,1)} %copy.80), calls=%async_computation.2 | async-start | bytes 4194304 | tf_op jit(solution)/shard_map/all_to_all | solution.py:76
  124.8 8.6 %gather_fusion.4 = bf16[256,128,128]{2,1,0:T(8,128)(2,1)} fusion(bf16[16,128,128]{2,1,0:T(8,128)(2,1)S(1)} %bitcast.68, s32[1024]{0:T(1024)S(1)} %pad_clamp_fusion.3), kind=kCustom, calls=%fused_computation.4 | custom fusion | bytes 16778240 | tf_op jit(solution)/shard_map/gather | solution.py:85
  136.8 42.5 %all-gather.2 = bf16[64,128]{1,0:T(8,128)(2,1)S(1)} all-gather(bf16[8,128]{1,0:T(8,128)(2,1)S(1)} %gather_fusion.6), channel_id=4, replica_groups=mesh['row'=4,'col'=8] {'col'}, dimensions={0}, use_global_device_ids=true | all-gather | bytes 18432 | tf_op jit(solution)/shard_map/all_gather | solution.py:90
  179.3 8.6 %all-gather.3 = bf16[256,128]{1,0:T(8,128)(2,1)S(1)} all-gather(bf16[64,128]{1,0:T(8,128)(2,1)S(1)} %all-gather.2), channel_id=5, replica_groups=mesh['row'=4,'col'=8] {'row'}, dimensions={0}, use_global_device_ids=true | all-gather | bytes 81920 | tf_op jit(solution)/shard_map/all_gather | solution.py:93
  187.9 7.4 %convolution_bitcast_fusion = bf16[256,128,128]{1,2,0:T(8,128)(2,1)S(1)} fusion(bf16[256,128,128]{2,1,0:T(8,128)(2,1)} %gather_fusion.4, bf16[256,128,128]{2,1,0:T(8,128)(2,1)} %param.12), kind=kOutput, calls=%fused_computation.9 | convolution fusion | flops 1073741824 | bytes 25165824 | tf_op jit(solution)/shard_map/tab,tas->tbs/dot_general | solution.py:84
  195.3 5.5 %fusion = f32[16,128,128]{1,0,2:T(8,128)} fusion(bf16[256,128,128]{1,2,0:T(8,128)(2,1)S(1)} %convolution_bitcast_fusion, bf16[256]{0:T(256)(128)(2,1)S(1)} %compare_convert_fusion.1, s32[256]{0:T(256)S(1)} %copy-done.6), kind=kOutput, calls=%fused_computation.7 | convolution fusion | flops 134225920 | bytes 9438720 | tf_op jit(solution)/shard_map/dt,tbs->dbs/dot_general | solution.py:87
  200.8 3.9 %fusion.5 = f32[16,16384]{1,0:T(8,128)} fusion(bf16[8,8,128,128]{3,2,1,0:T(8,128)(2,1)} %bitcast.26, s32[64]{0:T(128)S(1)} %eq.66), kind=kOutput, calls=%fused_computation.18 | convolution fusion | flops 33555456 | bytes 3145984 | tf_op jit(solution)/shard_map/dot_general | solution.py:88
  207.1 2.5 %copy.81 = f32[2048,128]{0,1:T(8,128)} copy(f32[2048,128]{1,0:T(8,128)} %reshape.120) | data formatting | bytes 2097152 | tf_op jit(solution)/shard_map/reshape | solution.py:99
  209.6 3.1 %fusion.4 = f32[2048,128]{0,1:T(8,128)} fusion(bf16[256,128]{1,0:T(8,128)(2,1)S(1)} %all-gather.3, bf16[256,2048]{1,0:T(8,128)(2,1)S(1)} %copy-done.4, f32[2048,128]{0,1:T(8,128)} %copy.81, f32[16,8,16,128]{3,2,1,0:T(8,128)} %bitcast.71), kind=kOutput, calls=%fused_computation.17 | convolution fusion | flops 135004160 | bytes 4259840 | tf_op jit(solution)/shard_map/dot_general | solution.py:91
  (58 shorter events, 30.9 us)
Async XLA Ops:
  0.6 17.5 %copy-start = (bf16[64,128,128]{2,1,0:T(8,128)(2,1)S(1)}, bf16[64,128,128]{2,1,0:T(8,128)(2,1)}, u32[]{:S(2)}) copy-start(bf16[64,128,128]{2,1,0:T(8,128)(2,1)} %param.16) | copy-start | bytes 6291460
  0.6 14.5 %copy-start.9 = (s32[64]{0:T(128)S(1)}, s32[64]{0:T(128)}, u32[]{:S(2)}) copy-start(s32[64]{0:T(128)} %param.17) | copy-start | bytes 772
  0.7 14.5 %copy-start.1 = (s32[1,32]{1,0:T(1,128)S(1)}, s32[1,32]{1,0:T(1,128)}, u32[]{:S(2)}) copy-start(s32[1,32]{1,0:T(1,128)} %param.19) | copy-start | bytes 388
  2.2 24.1 %all-to-all-start = ((s32[32,1,2]{2,1,0:T(1,128)}), s32[32,1,2]{2,1,0:T(1,128)S(1)}, u32[]{:S(2)}, u32[]{:S(2)}) async-start(s32[32,1,2]{2,1,0:T(1,128)} %bitcast.4), calls=%async_computation | async-start | bytes 32768 | tf_op jit(solution)/shard_map/all_to_all | solution.py:50
  11.1 2.7 %copy-start.2 = (f32[2048,128]{0,1:T(8,128)}, f32[2048,128]{0,1:T(8,128)S(1)}, u32[]{:S(2)}) copy-start(f32[2048,128]{0,1:T(8,128)S(1)} %copy.62) | copy-start | bytes 3145732
  22.1 10.1 %copy-start.5 = (bf16[2048,128]{0,1:T(8,128)(2,1)S(1)}, bf16[2048,128]{0,1:T(8,128)(2,1)}, u32[]{:S(2)}) copy-start(bf16[2048,128]{0,1:T(8,128)(2,1)} %get-tuple-element.13) | copy-start | bytes 1572868
  22.1 11.1 %copy-start.8 = (s32[256]{0:T(256)S(1)}, s32[256]{0:T(256)}, u32[]{:S(2)}) copy-start(s32[256]{0:T(256)} %param.13) | copy-start | bytes 3076
  26.3 70.5 %all-to-all-start.1 = ((bf16[32,2,128,128]{3,2,1,0:T(8,128)(2,1)}), bf16[32,2,128,128]{3,2,1,0:T(8,128)(2,1)}, u32[]{:S(2)}, u32[]{:S(2)}) async-start(bf16[32,2,128,128]{3,2,1,0:T(8,128)(2,1)} %copy.70), calls=%async_computation.1 | async-start | bytes 4194304 | tf_op jit(solution)/shard_map/all_to_all | solution.py:76
  51.2 12.9 %copy-start.6 = (s32[256]{0:T(256)S(1)}, s32[256]{0:T(256)}, u32[]{:S(2)}) copy-start(s32[256]{0:T(256)} %param.14) | copy-start | bytes 3076
  70.4 35.1 %copy-start.3 = (f32[2048,128]{0,1:T(8,128)S(1)}, f32[2048,128]{0,1:T(8,128)}, u32[]{:S(2)}) copy-start(f32[2048,128]{0,1:T(8,128)} %copy-done.2) | copy-start | bytes 3145732
  70.4 35.1 %copy-start.7 = (s32[128]{0:T(128)S(1)}, s32[128]{0:T(128)}, u32[]{:S(2)}) copy-start(s32[128]{0:T(128)} %param.23) | copy-start | bytes 1540
  121.3 79.5 %all-to-all-start.2 = ((bf16[32,2,128,128]{3,2,1,0:T(8,128)(2,1)}), bf16[32,2,128,128]{3,2,1,0:T(8,128)(2,1)}, u32[]{:S(2)}, u32[]{:S(2)}) async-start(bf16[32,2,128,128]{3,2,1,0:T(8,128)(2,1)} %copy.80), calls=%async_computation.2 | async-start | bytes 4194304 | tf_op jit(solution)/shard_map/all_to_all | solution.py:76
  200.8 8.8 %copy-start.4 = (bf16[256,2048]{1,0:T(8,128)(2,1)S(1)}, bf16[256,2048]{1,0:T(8,128)(2,1)}, u32[]{:S(2)}) copy-start(bf16[256,2048]{1,0:T(8,128)(2,1)} %param.21) | copy-start | bytes 3145732
where the time goes:
time: 217 us; the launch traced here: 215 us
  blocking collectives  74.3 us (34%)
  local copies, waits for them, and re-layouts  69.2 us (32%)
  matrix products  49 us (23%)
  starting transfers between devices  16.8 us (8%)
  other arithmetic  4.38 us (2%)
    all_gather x2, blocking collectives, body(): group_hubs = lax.all_gather(hub_state, 'col', axis=0, tiled=True)  57.1 us
    gather x2, local copies, waits for them, and re-layouts, body(): own_blocks[local_src]  17.2 us
    all_gather x2, blocking collectives, body(): lax.all_gather(group_hubs, 'row', axis=0, tiled=True)  17.2 us
    dot_general x2, matrix products, body(): jnp.einsum('tab,tas->tbs', local_tiles, own_blocks[local_src], preferred_...  16.8 us
    dot_general x1, local copies, waits for them, and re-layouts, body(): jnp.einsum('tab,tas->tbs', local_tiles, own_blocks[local_src], preferred_...  12.2 us
    dot_general x2, matrix products, body(): local_terms = jnp.einsum('dt,tbs->dbs', local_select, local_products)  10 us
    reshape x4, local copies, waits for them, and re-layouts, body(): remote_terms.reshape(vertex_rows, seed_count)  9.83 us
    all_to_all x2, starting transfers between devices, body(): lax.all_to_all(outgoing.reshape(device_count, capacity, tile_size, seed_c...  9.45 us
  transfers between devices with their start and end apart: 3, of which 0 were waited for; matrix products, arithmetic and copies ran while one was open for 38% of the time, Pallas kernels for 0%

commit v1 on v0

v1 whole, which is shorter than its diff:
```python
import functools

import jax
import jax.numpy as jnp
from jax import lax
from jax.experimental import pallas as pl
from jax.experimental.pallas import tpu as pltpu
from jax.sharding import PartitionSpec as P

DAMPING = 0.85
AXES = ("row", "col")
VMEM = pl.BlockSpec(memory_space=pltpu.VMEM)
SMEM = pl.BlockSpec(memory_space=pltpu.SMEM)
TAIL = 16
LIMIT = 56 * 1024 * 1024


def teleport_block(prior, seeds, block, tile):
    rows = lax.broadcasted_iota(jnp.int32, (tile, prior.shape[1]), 0) + block * tile
    return prior[pl.ds(block * tile, tile), :] + jnp.where(rows == seeds[...], 4.0, 0.0)


def push(src, dst, live, hubs, tiles, work, hub_rows, state, out):
    slots, tile, _ = tiles.shape
    blocks = state.shape[0]
    devices = live.shape[1]
    cap = slots // devices
    hub_dev = hubs.shape[0]
    for h in range(hub_dev):
        hub_rows[pl.ds(h, 1), :] = work[pl.ds(hubs[h], 1), :]
    for h in range(hub_dev):
        work[pl.ds(hubs[h], 1), :] = jnp.zeros((1, work.shape[1]), jnp.float32)

    def turn(block, carry):
        state[block] = work[pl.ds(block * tile, tile), :].T.astype(jnp.bfloat16)
        return carry

    lax.fori_loop(0, blocks, turn, 0, unroll=4)

    def send(k, carry):
        tail = hub_rows[...]
        rows = lax.broadcasted_iota(jnp.int32, tail.shape, 0)
        for c in range(cap):
            tail = jnp.where(rows == hub_dev + c, dst[k * cap + c].astype(jnp.float32), tail)
        out[k, cap * tile :, :] = tail.astype(jnp.bfloat16)
        for c in range(cap):
            j = k * cap + c
            value = jnp.dot(state[src[j]], tiles[j], preferred_element_type=jnp.float32)
            value = jnp.where(live[0, k] > c, value, 0.0)
            out[k, c * tile : (c + 1) * tile, :] = value.astype(jnp.bfloat16)
        return carry

    lax.fori_loop(0, devices, send, 0, unroll=4)


def first_kernel(src, dst, live, hubs, seeds, prior, tiles, out, state, work, hub_rows):
    tile = tiles.shape[1]

    def begin(block, carry):
        work[pl.ds(block * tile, tile), :] = teleport_block(prior, seeds, block, tile)
        return carry

    lax.fori_loop(0, state.shape[0], begin, 0, unroll=4)
    hub_rows[...] = jnp.zeros_like(hub_rows)
    push(src, dst, live, hubs, tiles, work, hub_rows, state, out)


def local_kernel(src, dst, count, tiles, state, total):
    step = pl.program_id(0)
    chunk = tiles.shape[0]
    unroll = 8

    @pl.when(step == 0)
    def _():
        total[...] = jnp.zeros_like(total)

    first = step * chunk
    here = jnp.clip(count[0] - first, 0, chunk)

    def several(i, carry):
        values = []
        for u in range(unroll):
            t = i * unroll + u
            values.append(
                jnp.dot(state[src[first + t]], tiles[t], preferred_element_type=jnp.float32)
            )
        for u in range(unroll):
            t = i * unroll + u
            total[dst[first + t]] += jnp.where(t < here, values[u], 0.0)
        return carry

    lax.fori_loop(0, (here + unroll - 1) // unroll, several, 0)


def gather_terms(incoming, targets, total, acc):
    devices = incoming.shape[0]
    tile = total.shape[1]
    cap = targets.shape[0] // devices
    acc[...] = total[...]

    def add(k, carry):
        for c in range(cap):
            part = incoming[k, c * tile : (c + 1) * tile, :].astype(jnp.float32)
            acc[targets[k * cap + c]] += part
        return carry

    lax.fori_loop(0, devices, add, 0, unroll=2)


def hub_states(incoming, hub_all, hub_dev, cap, ints=None):
    devices, rows, _ = incoming.shape

    def take(k, carry):
        tail = incoming[k, rows - TAIL :, :].astype(jnp.float32)
        hub_all[pl.ds(k * hub_dev, hub_dev), :] = tail[:hub_dev]
        if ints is not None:
            ints[pl.ds(k * 8, 8), :] = tail[hub_dev : hub_dev + 8].astype(jnp.int32)
        return carry

    lax.fori_loop(0, devices, take, 0, unroll=4)
    return hub_all[...].T.astype(jnp.bfloat16)


def middle_kernel(
    src, dst, live, hubs, seeds, prior, tiles, incoming, total, weights,
    out, state, rank, targets, work, hub_rows, acc, hub_all, ints, ints_smem, sem,
):
    tile = tiles.shape[1]
    blocks = state.shape[0]
    devices = live.shape[1]
    cap = tiles.shape[0] // devices
    hub_dev = hubs.shape[0]
    hub_state = hub_states(incoming, hub_all, hub_dev, cap, ints)
    copy = pltpu.make_async_copy(ints, ints_smem, sem)
    copy.start()
    copy.wait()
    for c in range(cap):

        def fill(k, carry, c=c):
            targets[k * cap + c] = ints_smem[k * 8 + c, 0]
            return carry

        lax.fori_loop(0, devices, fill, 0, unroll=8)
    gather_terms(incoming, targets, total, acc)
    for block in range(blocks):
        rows = pl.ds(block * tile, tile)
        hub = jnp.dot(hub_state, weights[:, rows], preferred_element_type=jnp.float32)
        residual = (DAMPING * (acc[block] + hub)).T
        work[rows, :] = residual
        rank[rows, :] = (1.0 - DAMPING) * teleport_block(prior, seeds, block, tile) + (
            1.0 - DAMPING
        ) * residual
    hub_rows[...] = jnp.zeros_like(hub_rows)
    push(src, dst, live, hubs, tiles, work, hub_rows, state, out)


def last_kernel(hub_dev, targets, incoming, total, weights, residual, acc, hub_all):
    blocks, tile, _ = total.shape
    cap = targets.shape[0] // incoming.shape[0]
    hub_state = hub_states(incoming, hub_all, hub_dev, cap)
    gather_terms(incoming, targets, total, acc)
    for block in range(blocks):
        rows = pl.ds(block * tile, tile)
        hub = jnp.dot(hub_state, weights[:, rows], preferred_element_type=jnp.float32)
        residual[rows, :] = (DAMPING * (acc[block] + hub)).T


def body(
    local_tiles, local_src, local_dst, local_count, remote_tiles, remote_src,
    remote_dst, bucket_count, hub_ids, hub_weights, prior, seed_ids,
):
    devices = lax.axis_size(AXES)
    own = lax.axis_index(AXES)
    vertex_rows, seeds = prior.shape
    tile = local_tiles.shape[1]
    blocks = vertex_rows // tile
    slots = remote_src.shape[0]
    cap = slots // devices
    hub_dev = hub_ids.shape[0]
    local_slots = local_src.shape[0]
    rows = cap * tile + TAIL
    hubs = hub_ids - own * vertex_rows
    seed_rows = (seed_ids - own * vertex_rows).reshape(1, seeds)

    f32, bf16, i32 = jnp.float32, jnp.bfloat16, jnp.int32
    payload = jax.ShapeDtypeStruct((devices, rows, seeds), bf16)
    state_shape = jax.ShapeDtypeStruct((blocks, seeds, tile), bf16)
    total_shape = jax.ShapeDtypeStruct((blocks, seeds, tile), f32)
    vertex_shape = jax.ShapeDtypeStruct((vertex_rows, seeds), f32)
    work = pltpu.VMEM((vertex_rows, seeds), f32)
    hub_rows = pltpu.VMEM((TAIL, seeds), f32)
    acc = pltpu.VMEM((blocks, seeds, tile), f32)
    hub_all = pltpu.VMEM((devices * hub_dev, seeds), f32)
    params = pltpu.CompilerParams(vmem_limit_bytes=LIMIT)

    out, state = pl.pallas_call(
        first_kernel,
        out_shape=(payload, state_shape),
        in_specs=[SMEM] * 4 + [VMEM] * 3,
        out_specs=(VMEM, VMEM),
        scratch_shapes=[work, hub_rows],
        compiler_params=params,
    )(remote_src, remote_dst, bucket_count, hubs, seed_rows, prior, remote_tiles)

    def exchange(array):
        return lax.all_to_all(array, AXES, split_axis=0, concat_axis=0, tiled=True)

    chunk = 32

    def local(state):
        return pl.pallas_call(
            local_kernel,
            grid=(local_slots // chunk,),
            out_shape=total_shape,
            in_specs=[SMEM, SMEM, SMEM]
            + [
                pl.BlockSpec((chunk, tile, tile), lambda i: (i, 0, 0)),
                pl.BlockSpec((blocks, seeds, tile), lambda i: (0, 0, 0)),
            ],
            out_specs=pl.BlockSpec((blocks, seeds, tile), lambda i: (0, 0, 0)),
            compiler_params=params,
            cost_estimate=pl.CostEstimate(
                flops=2 * local_slots * tile * tile * seeds,
                bytes_accessed=local_slots * tile * tile * 2,
                transcendentals=0,
            ),
        )(local_src, local_dst, local_count, local_tiles, state)

    incoming = exchange(out)
    total = local(state)
    out, state, rank, targets = pl.pallas_call(
        middle_kernel,
        out_shape=(payload, state_shape, vertex_shape, jax.ShapeDtypeStruct((slots,), i32)),
        in_specs=[SMEM] * 4 + [VMEM] * 6,
        out_specs=(VMEM, VMEM, VMEM, SMEM),
        scratch_shapes=[
            work, hub_rows, acc, hub_all,
            pltpu.VMEM((devices * 8, seeds), i32),
            pltpu.SMEM((devices * 8, seeds), i32),
            pltpu.SemaphoreType.DMA,
        ],
        compiler_params=params,
    )(
        remote_src, remote_dst, bucket_count, hubs, seed_rows, prior, remote_tiles,
        incoming, total, hub_weights,
    )
    incoming = exchange(out)
    total = local(state)
    residual = pl.pallas_call(
        functools.partial(last_kernel, hub_dev),
        out_shape=vertex_shape,
        in_specs=[SMEM] + [VMEM] * 3,
        out_specs=VMEM,
        scratch_shapes=[acc, hub_all],
        compiler_params=params,
    )(targets, incoming, total, hub_weights)
    return rank, residual


def solution(mesh):
    both = P(AXES)
    placed = (
        P(AXES, None, None), both, both, both, P(AXES, None, None), both,
        both, P(AXES, None), both, P(None, AXES), P(AXES, None), P(),
    )
    return jax.shard_map(
        body,
        mesh=mesh,
        in_specs=placed,
        out_specs=(P(AXES, None), P(AXES, None)),
        check_vma=False,
    )
```

time: 217 us -> 143 us (0.66)
  waiting for transfers between devices: 0.01 us -> 84.9 us
  blocking collectives: 74.3 us -> 0 us
  local copies, waits for them, and re-layouts: 69.2 us -> 2.71 us
  matrix products: 49 us -> 0 us
  Pallas kernels: 0 us -> 41.3 us
  starting transfers between devices: 16.8 us -> 10.1 us
    all_to_all x3 -> x2, waiting for transfers between devices: 0.01 us -> 84.9 us  [exchange(): return lax.all_to_all(array, AXES, split_axis=0, concat_axis=0, tiled=True)]
    all_gather x4 -> x0, blocking collectives: 74.3 us -> none  [the longest x2 57.1 us: body(): group_hubs = lax.all_gather(hub_state, 'col', axis=0, tiled=True)]
    dot_general x10 -> x0, matrix products: 49 us -> none  [the longest x2 16.8 us: body(): jnp.einsum('tab,tas->tbs', local_tiles, own_blocks[local_src], preferred_...]
    pallas_call x0 -> x5, Pallas kernels: none -> 41.3 us  [the longest x2 20.2 us: local(): pl.pallas_call(local_kernel, grid=(local_slots // chunk,), out_shape=tota...]
    gather x7 -> x0, local copies, waits for them, and re-layouts: 24.6 us -> none  [the longest x2 17.2 us: body(): own_blocks[local_src]]
    reshape x9 -> x0, local copies, waits for them, and re-layouts: 22 us -> none  [the longest x4 9.83 us: body(): remote_terms.reshape(vertex_rows, seed_count)]
    dot_general x2 -> x0, local copies, waits for them, and re-layouts: 12.6 us -> none  [the longest x1 12.2 us: body(): jnp.einsum('tab,tas->tbs', local_tiles, own_blocks[local_src], preferred_...]
    all_to_all x3 -> x2, starting transfers between devices: 16.8 us -> 10.1 us  [exchange(): return lax.all_to_all(array, AXES, split_axis=0, concat_axis=0, tiled=True)]
  transfers between devices with their start and end apart: 3 -> 2, of which waited for: 0 -> 2; matrix products, arithmetic and copies ran while one was open for 38% -> 0% of each run, Pallas kernels for 0% -> 14%
where the time goes in v1:
time: 143 us
  waiting for transfers between devices  84.9 us (59%)
  Pallas kernels  41.3 us (29%)
  starting transfers between devices  10.1 us (7%)
  local copies, waits for them, and re-layouts  2.71 us (2%)
  other arithmetic  2.43 us (2%)
    all_to_all x2, waiting for transfers between devices, exchange(): return lax.all_to_all(array, AXES, split_axis=0, concat_axis=0, tiled=True)  84.9 us
    pallas_call x2, Pallas kernels, local(): pl.pallas_call(local_kernel, grid=(local_slots // chunk,), out_shape=tota...  20.2 us
    pallas_call x1, Pallas kernels, body(): pl.pallas_call(middle_kernel, out_shape=(payload, state_shape, vertex_sha...  11.1 us
    all_to_all x2, starting transfers between devices, exchange(): return lax.all_to_all(array, AXES, split_axis=0, concat_axis=0, tiled=True)  10.1 us
    pallas_call x1, Pallas kernels, body(): pl.pallas_call(first_kernel, out_shape=(payload, state_shape), in_specs=[...  5.67 us
    pallas_call x1, Pallas kernels, body(): pl.pallas_call(functools.partial(last_kernel, hub_dev), out_shape=vertex_...  4.32 us
  transfers between devices with their start and end apart: 2, of which 2 were waited for; matrix products, arithmetic and copies ran while one was open for 0% of the time, Pallas kernels for 14%

profile of v1, /device:TPU:0, one launch (start us, length us, event | category | flops | bytes accessed | tf_op | source)
XLA Modules:
  0.0 142.8 jit_solution(6071491705302181950)
XLA Ops:
  0.6 1.2 broadcast_subtract_fusion.hubs
  1.8 1.2 subtract_bitcast_fusion.seeds
  3.1 5.7 %shard_map.131 = (bf16[32,272,128]{2,1,0:T(8,128)(2,1)}, bf16[16,128,128]{2,1,0:T(8,128)(2,1)}) custom-call(s32[64]{0:T(128)} %src.6, s32[64]{0:T(128)} %dst.6, s32[1,32]{1,0:T(1,128)} %live.3, s32[8]{0:T(128)} %broadcast_subtract_fusion.hubs, s32[1,128]{1,0:T(1,128)} %subtract_bitcast_fusion.seeds, f32[2048,128]{1,0:T(8,128)} %prior.3, ...), custom_call_target="tpu_custom_call" | custom-call | tf_op jit(solution)/shard_map/pallas_call | solution.py:196
  8.7 7.3 %all-to-all-start = ((bf16[32,272,128]{2,1,0:T(8,128)(2,1)}), bf16[32,272,128]{2,1,0:T(8,128)(2,1)S(1)}, u32[]{:S(2)}, u32[]{:S(2)}) async-start(bf16[32,272,128]{2,1,0:T(8,128)(2,1)} %get-tuple-element.8), calls=%async_computation | async-start | bytes 4456448 | tf_op jit(solution)/shard_map/all_to_all | solution.py:206
  16.7 10.1 %shard_map.132.total = f32[16,128,128]{2,1,0:T(8,128)} custom-call(s32[256]{0:T(256)} %src.7, s32[256]{0:T(256)} %dst.7, s32[1]{0:T(128)S(6)} %copy.14.count, bf16[256,128,128]{2,1,0:T(8,128)(2,1)} %tiles.7, bf16[16,128,128]{2,1,0:T(8,128)(2,1)} %get-tuple-element.9.state), custom_call_target="tpu_custom_call" | custom-call | flops 1073741824 | bytes 8388608 | tf_op jit(solution)/shard_map/pallas_call | solution.py:211
  26.8 42.1 %all-to-all-done.incoming = bf16[32,272,128]{2,1,0:T(8,128)(2,1)S(1)} async-done(((bf16[32,272,128]{2,1,0:T(8,128)(2,1)}), bf16[32,272,128]{2,1,0:T(8,128)(2,1)S(1)}, u32[]{:S(2)}, u32[]{:S(2)}) %all-to-all-start) | async-done | bytes 2228256 | tf_op jit(solution)/shard_map/all_to_all | solution.py:206
  69.0 0.0 copy-start
  69.0 1.3 copy-done
  70.3 11.1 %shard_map.133 = (bf16[32,272,128]{2,1,0:T(8,128)(2,1)}, bf16[16,128,128]{2,1,0:T(8,128)(2,1)}, f32[2048,128]{1,0:T(8,128)}, s32[64]{0:T(128)}) custom-call(s32[64]{0:T(128)} %src.6, s32[64]{0:T(128)} %dst.6, s32[1,32]{1,0:T(1,128)} %live.3, s32[8]{0:T(128)} %broadcast_subtract_fusion.hubs, s32[1,128]{1,0:T(1,128)} %subtract_bitcast_fusion.seeds, ...), custom_call_target="tpu_custom_call" | custom-call | tf_op jit(solution)/shard_map/pallas_call | solution.py:231
  81.4 2.8 %all-to-all-start.1 = ((bf16[32,272,128]{2,1,0:T(8,128)(2,1)}), bf16[32,272,128]{2,1,0:T(8,128)(2,1)S(1)}, u32[]{:S(2)}, u32[]{:S(2)}) async-start(bf16[32,272,128]{2,1,0:T(8,128)(2,1)} %get-tuple-element.12), calls=%async_computation.1 | async-start | bytes 4456448 | tf_op jit(solution)/shard_map/all_to_all | solution.py:206
  84.2 10.1 %shard_map.134.total = f32[16,128,128]{2,1,0:T(8,128)} custom-call(s32[256]{0:T(256)} %src.7, s32[256]{0:T(256)} %dst.7, s32[1]{0:T(128)S(6)} %copy.14.count, bf16[256,128,128]{2,1,0:T(8,128)(2,1)} %tiles.7, bf16[16,128,128]{2,1,0:T(8,128)(2,1)} %get-tuple-element.13.state), custom_call_target="tpu_custom_call" | custom-call | flops 1073741824 | bytes 8388608 | tf_op jit(solution)/shard_map/pallas_call | solution.py:211
  94.3 42.8 %all-to-all-done.1.incoming = bf16[32,272,128]{2,1,0:T(8,128)(2,1)S(1)} async-done(((bf16[32,272,128]{2,1,0:T(8,128)(2,1)}), bf16[32,272,128]{2,1,0:T(8,128)(2,1)S(1)}, u32[]{:S(2)}, u32[]{:S(2)}) %all-to-all-start.1) | async-done | bytes 2228256 | tf_op jit(solution)/shard_map/all_to_all | solution.py:206
  137.1 0.0 copy-start.1
  137.1 1.4 copy-done.1
  138.5 4.3 %shard_map.135 = f32[2048,128]{1,0:T(8,128)} custom-call(s32[64]{0:T(128)} %get-tuple-element.11.targets, bf16[32,272,128]{2,1,0:T(8,128)(2,1)} %copy-done.1, f32[16,128,128]{2,1,0:T(8,128)} %shard_map.134.total, bf16[256,2048]{1,0:T(8,128)(2,1)} %weights.3), custom_call_target="tpu_custom_call" | custom-call | tf_op jit(solution)/shard_map/pallas_call | solution.py:249
Async XLA Ops:
  8.7 60.2 %all-to-all-start = ((bf16[32,272,128]{2,1,0:T(8,128)(2,1)}), bf16[32,272,128]{2,1,0:T(8,128)(2,1)S(1)}, u32[]{:S(2)}, u32[]{:S(2)}) async-start(bf16[32,272,128]{2,1,0:T(8,128)(2,1)} %get-tuple-element.8), calls=%async_computation | async-start | bytes 4456448 | tf_op jit(solution)/shard_map/all_to_all | solution.py:206
  69.0 1.3 copy-start
  81.4 55.7 %all-to-all-start.1 = ((bf16[32,272,128]{2,1,0:T(8,128)(2,1)}), bf16[32,272,128]{2,1,0:T(8,128)(2,1)S(1)}, u32[]{:S(2)}, u32[]{:S(2)}) async-start(bf16[32,272,128]{2,1,0:T(8,128)(2,1)} %get-tuple-element.12), calls=%async_computation.1 | async-start | bytes 4456448 | tf_op jit(solution)/shard_map/all_to_all | solution.py:206
  137.1 1.4 copy-start.1

commit v2 on v0

v2 whole, which is shorter than its diff:
```python
import functools

import jax
import jax.numpy as jnp
from jax import lax
from jax.experimental import pallas as pl
from jax.experimental.pallas import tpu as pltpu
from jax.sharding import PartitionSpec as P

DAMPING = 0.85
ITERS = 2
AXES = ("row", "col")
VMEM = pl.BlockSpec(memory_space=pltpu.VMEM)
SMEM = pl.BlockSpec(memory_space=pltpu.SMEM)
ANY = pl.BlockSpec(memory_space=pl.ANY)
TAIL = 16
LIMIT = 62 * 1024 * 1024
MESH = pl.DeviceIdType.MESH
f32, bf16, i32 = jnp.float32, jnp.bfloat16, jnp.int32


def iota(shape, axis):
    return lax.broadcasted_iota(i32, shape, axis)


def sort_tables(keys, blocks):
    n = keys.shape[0]
    index = jnp.arange(n, dtype=i32)
    row, column = keys[None, :], keys[:, None]
    before = (row < column) | ((row == column) & (index[None, :] < index[:, None]))
    place = jnp.sum(before.astype(i32), axis=1)
    hit = place[:, None] == index[None, :]
    order = jnp.sum(jnp.where(hit, index[:, None], 0), axis=0)
    starts = jnp.sum((column < jnp.arange(blocks + 1, dtype=i32)[None, :]).astype(i32), axis=0)
    return order, starts


def kernel(
    n_col, cap, src, live, hubs, lsrc, lorder, lstart, rdev, rslot, rstart, seeds, prior,
    weights, tiles, ltiles,
    rank, res, out, recv_first, recv_last, state, lt, sums, total, hub_rows, hub_all,
    send_sem, recv_sem, tile_sem,
):
    recvs = (recv_first, recv_last)
    devices = live.shape[1]
    slots, tile, _ = tiles.shape
    vertex_rows, columns = prior.shape
    blocks = vertex_rows // tile
    half = columns // 2
    hub_dev = hubs.shape[0]
    local_slots = lt.shape[0]
    me = lax.axis_index("row") * n_col + lax.axis_index("col")
    base = me * vertex_rows

    fetch = pltpu.make_async_copy(ltiles, lt, tile_sem)
    fetch.start()

    def device(k):
        return (k // n_col, k % n_col)

    barrier = pltpu.get_barrier_semaphore()

    def greet(o, carry):
        k = lax.rem(me + o, devices)
        pl.semaphore_signal(barrier, inc=1, device_id=device(k), device_id_type=MESH)
        return carry

    lax.fori_loop(1, devices, greet, 0)

    def teleport(block):
        rows = iota((tile, columns), 0) + (base + block * tile)
        return prior[pl.ds(block * tile, tile), :] + jnp.where(rows == seeds[...], 4.0, 0.0)

    def begin(block, carry):
        res[pl.ds(block * tile, tile), :] = teleport(block)
        return carry

    lax.fori_loop(0, blocks, begin, 0, unroll=4)
    hub_rows[...] = jnp.zeros_like(hub_rows)

    def partner_copy(r, o):
        k = lax.rem(me + o, devices)
        return pltpu.make_async_remote_copy(
            src_ref=out.at[k],
            dst_ref=recvs[r].at[me],
            send_sem=send_sem.at[r, o],
            recv_sem=recv_sem.at[r, o],
            device_id=device(k),
            device_id_type=MESH,
        )

    for r in range(ITERS):
        def turn(block, found):
            rows = iota((tile, columns), 0) + (base + block * tile)
            value = res[pl.ds(block * tile, tile), :]
            is_hub = rows == hubs[0]
            for h in range(1, hub_dev):
                is_hub = is_hub | (rows == hubs[h])
            state[block] = jnp.where(is_hub, 0.0, value).T.astype(bf16)
            more = []
            for h in range(hub_dev):
                part = jnp.where(rows == hubs[h], value, 0.0).reshape(tile // 8, 8, columns)
                more.append(found[h] + jnp.sum(part, axis=0))
            return tuple(more)

        nothing = tuple(jnp.zeros((8, columns), f32) for h in range(hub_dev))
        found = lax.fori_loop(0, blocks, turn, nothing)
        for h in range(hub_dev):
            hub_rows[h : h + 1, :] = jnp.sum(found[h], axis=0, keepdims=True)

        def payload(k, store):
            store(cap * tile, TAIL, hub_rows[...].astype(bf16))
            for c in range(cap):
                j = k * cap + c
                value = jnp.dot(state[src[j]], tiles[j], preferred_element_type=f32)
                value = value * (live[0, k] > c).astype(f32)
                store(c * tile, tile, value.astype(bf16))

        if r == 0:
            pl.semaphore_wait(barrier, devices - 1)

        def send(o, carry, r=r):
            k = lax.rem(me + o, devices)

            def store(at, size, value):
                out[k, at : at + size, :] = value

            payload(k, store)
            partner_copy(r, o).start()
            return carry

        lax.fori_loop(1, devices, send, 0)

        def keep(at, size, value, r=r):
            recvs[r][me, at : at + size, :] = value

        payload(me, keep)

        if r == 0:
            fetch.wait()

        def finish(start, h, add):
            for d in range(blocks):
                value = sums[start[d + 1]] - sums[start[d]]
                where = slice(h * half, (h + 1) * half)
                if add:
                    total[d, where, :] += value
                else:
                    total[d, where, :] = value

        sums[0] = jnp.zeros((half, tile), f32)
        for h in range(2):

            def local(t, acc, h=h):
                p = lorder[t]
                left = state[lsrc[p], h * half : (h + 1) * half, :]
                acc = acc + jnp.dot(left, lt[p], preferred_element_type=f32)
                sums[t + 1] = acc
                return acc

            lax.fori_loop(0, local_slots, local, jnp.zeros((half, tile), f32), unroll=8)
            finish(lstart, h, False)

        def arrive(o, carry, r=r):
            partner_copy(r, o).wait()
            return carry

        lax.fori_loop(1, devices, arrive, 0)

        def take(k, carry, r=r):
            tail = recvs[r][k, cap * tile :, :].astype(f32)
            hub_all[pl.ds(k * hub_dev, hub_dev), :] = tail[:hub_dev]
            return carry

        lax.fori_loop(0, devices, take, 0, unroll=4)
        for h in range(2):

            def remote(t, acc, h=h, r=r):
                part = 0.0
                for c in range(cap):
                    at = c * tile + h * half
                    here = recvs[r][rdev[t], at : at + half, :].astype(f32)
                    part = part + here * (rslot[t] == c).astype(f32)
                acc = acc + part
                sums[t + 1] = acc
                return acc

            lax.fori_loop(0, slots, remote, jnp.zeros((half, tile), f32), unroll=8)
            finish(rstart, h, True)

        hub_state = hub_all[...].T.astype(bf16)

        def combine(block, carry, r=r, hub_state=hub_state):
            rows = pl.ds(pl.multiple_of(block * tile, tile), tile)
            hub = jnp.dot(hub_state, weights[:, rows], preferred_element_type=f32)
            residual = (DAMPING * (total[block] + hub)).T
            if r == 0:
                rank[rows, :] = (1.0 - DAMPING) * teleport(block) + (1.0 - DAMPING) * residual
            res[rows, :] = residual
            return carry

        lax.fori_loop(0, blocks, combine, 0, unroll=2)


def body(
    n_col, local_tiles, local_src, local_dst, local_count, remote_tiles, remote_src,
    remote_dst, bucket_count, hub_ids, hub_weights, prior, seed_ids,
):
    devices = lax.axis_size(AXES)
    vertex_rows, columns = prior.shape
    tile = local_tiles.shape[1]
    blocks = vertex_rows // tile
    slots = remote_src.shape[0]
    cap = slots // devices
    hub_dev = hub_ids.shape[0]
    local_slots = local_src.shape[0]
    rows = cap * tile + TAIL
    vertex = jax.ShapeDtypeStruct((vertex_rows, columns), f32)
    targets = lax.all_to_all(
        remote_dst.reshape(devices, cap), AXES, split_axis=0, concat_axis=0, tiled=True
    ).reshape(-1)
    living = jnp.arange(local_slots, dtype=i32) < local_count[0]
    lorder, lstart = sort_tables(jnp.where(living, local_dst, blocks), blocks)
    rorder, rstart = sort_tables(targets, blocks)
    return pl.pallas_call(
        functools.partial(kernel, n_col, cap),
        out_shape=(vertex, vertex),
        in_specs=[SMEM] * 9 + [VMEM] * 4 + [ANY],
        out_specs=(VMEM, VMEM),
        scratch_shapes=[
            pltpu.VMEM((devices, rows, columns), bf16),
            pltpu.VMEM((devices, rows, columns), bf16),
            pltpu.VMEM((devices, rows, columns), bf16),
            pltpu.VMEM((blocks, columns, tile), bf16),
            pltpu.VMEM(local_tiles.shape, bf16),
            pltpu.VMEM((max(local_slots, slots) + 1, columns // 2, tile), f32),
            pltpu.VMEM((blocks, columns, tile), f32),
            pltpu.VMEM((TAIL, columns), f32),
            pltpu.VMEM((devices * hub_dev, columns), f32),
            pltpu.SemaphoreType.DMA((ITERS, devices)),
            pltpu.SemaphoreType.DMA((ITERS, devices)),
            pltpu.SemaphoreType.DMA,
        ],
        compiler_params=pltpu.CompilerParams(
            collective_id=0, has_side_effects=True, vmem_limit_bytes=LIMIT
        ),
    )(
        remote_src, bucket_count, hub_ids, local_src, lorder, lstart, rorder // cap, rorder % cap,
        rstart, seed_ids.reshape(1, columns), prior,
        hub_weights, remote_tiles, local_tiles,
    )


def solution(mesh):
    both = P(AXES)
    placed = (
        P(AXES, None, None), both, both, both, P(AXES, None, None), both,
        both, P(AXES, None), both, P(None, AXES), P(AXES, None), P(),
    )
    return jax.shard_map(
        functools.partial(body, mesh.shape["col"]),
        mesh=mesh,
        in_specs=placed,
        out_specs=(P(AXES, None), P(AXES, None)),
        check_vma=False,
    )
```

time: 217 us -> 138 us (0.64)
  Pallas kernels: 0 us -> 113 us
  blocking collectives: 74.3 us -> 0 us
  local copies, waits for them, and re-layouts: 69.2 us -> 6.5 us
  matrix products: 49 us -> 0 us
  starting transfers between devices: 16.8 us -> 7.3 us
  waiting for transfers between devices: 0.01 us -> 4.23 us
    pallas_call x0 -> x1, Pallas kernels: none -> 113 us  [body(): pl.pallas_call(functools.partial(kernel, n_col, cap), out_shape=(vertex,...]
    all_gather x4 -> x0, blocking collectives: 74.3 us -> none  [the longest x2 57.1 us: body(): group_hubs = lax.all_gather(hub_state, 'col', axis=0, tiled=True)]
    dot_general x10 -> x0, matrix products: 49 us -> none  [the longest x2 16.8 us: body(): jnp.einsum('tab,tas->tbs', local_tiles, own_blocks[local_src], preferred_...]
    gather x7 -> x0, local copies, waits for them, and re-layouts: 24.6 us -> none  [the longest x2 17.2 us: body(): own_blocks[local_src]]
    reshape x9 -> x0, local copies, waits for them, and re-layouts: 22 us -> none  [the longest x4 9.83 us: body(): remote_terms.reshape(vertex_rows, seed_count)]
    dot_general x2 -> x0, local copies, waits for them, and re-layouts: 12.6 us -> none  [the longest x1 12.2 us: body(): jnp.einsum('tab,tas->tbs', local_tiles, own_blocks[local_src], preferred_...]
    all_to_all x3 -> x1, starting transfers between devices: 16.8 us -> 7.3 us  [body(): lax.all_to_all(remote_dst.reshape(devices, cap), AXES, split_axis=0, conc...]
    all_to_all x3 -> x1, waiting for transfers between devices: 0.01 us -> 4.23 us  [body(): lax.all_to_all(remote_dst.reshape(devices, cap), AXES, split_axis=0, conc...]
  transfers between devices with their start and end apart: 3 -> 1, of which waited for: 0 -> 1; matrix products, arithmetic and copies ran while one was open for 38% -> 2% of each run, Pallas kernels for 0% -> 0%
where the time goes in v2:
time: 138 us; the launch traced here: 137 us
  Pallas kernels  113 us (82%)
  starting transfers between devices  7.3 us (5%)
  local copies, waits for them, and re-layouts  6.5 us (5%)
  other arithmetic  4.36 us (3%)
  waiting for transfers between devices  4.23 us (3%)
    pallas_call x1, Pallas kernels, body(): pl.pallas_call(functools.partial(kernel, n_col, cap), out_shape=(vertex,...  113 us
    all_to_all x1, starting transfers between devices, body(): lax.all_to_all(remote_dst.reshape(devices, cap), AXES, split_axis=0, conc...  7.3 us
    unnamed x2, local copies, waits for them, and re-layouts  4.52 us
    all_to_all x1, waiting for transfers between devices, body(): lax.all_to_all(remote_dst.reshape(devices, cap), AXES, split_axis=0, conc...  4.23 us
  transfers between devices with their start and end apart: 1, of which 1 were waited for; matrix products, arithmetic and copies ran while one was open for 2% of the time, Pallas kernels for 0%

profile of v2, /device:TPU:0, one launch (start us, length us, event | category | flops | bytes accessed | tf_op | source)
XLA Modules:
  0.0 136.8 jit_solution(16537337749465686726)
XLA Ops:
  0.6 1.4 all_to_all.6
  2.0 7.3 %all-to-all-start = ((s32[32,1,2]{2,1,0:T(1,128)}), s32[32,1,2]{2,1,0:T(1,128)S(1)}, u32[]{:S(2)}, u32[]{:S(2)}) async-start(s32[32,1,2]{2,1,0:T(1,128)} %bitcast.1), calls=%async_computation | async-start | bytes 32768 | tf_op jit(solution)/shard_map/all_to_all | solution.py:219
  9.9 0.7 compare_select_fusion
  10.6 0.2 convert_reduce_fusion
  10.8 0.7 select_reduce_fusion.lorder
  11.5 0.6 convert_reduce_fusion.2.lstart
  12.1 4.2 %all-to-all-done = s32[32,1,2]{2,1,0:T(1,128)S(1)} async-done(((s32[32,1,2]{2,1,0:T(1,128)}), s32[32,1,2]{2,1,0:T(1,128)S(1)}, u32[]{:S(2)}, u32[]{:S(2)}) %all-to-all-start) | async-done | bytes 288 | tf_op jit(solution)/shard_map/all_to_all | solution.py:219
  16.4 0.5 broadcast.31
  16.9 0.7 reduce.3
  17.6 0.1 lt.113
  17.7 0.6 convert_reduce_fusion.3.rstart
  18.3 0.2 convert_reduce_fusion.1
  18.5 0.1 select_reduce_fusion.1
  18.6 0.6 and_select_fusion
  19.2 113.1 %shard_map.131 = (f32[2048,128]{1,0:T(8,128)}, f32[2048,128]{1,0:T(8,128)}) custom-call(s32[64]{0:T(128)} %src.1, s32[1,32]{1,0:T(1,128)} %live.1, s32[8]{0:T(128)} %hubs.1, s32[256]{0:T(256)} %lsrc.1, s32[256]{0:T(256)} %select_reduce_fusion.lorder, s32[17]{0:T(128)} %convert_reduce_fusion.2.lstart, s32[64]{0:T(128)} %get-tuple-element.3.rdev, ...), custom_call_target="tpu_custom_call" | custom-call | tf_op jit(solution)/shard_map/pallas_call | solution.py:225
  132.2 2.3 %copy.19 = f32[2048,128]{1,0:T(8,128)} copy(f32[2048,128]{1,0:T(8,128)} %get-tuple-element.6) | data formatting | bytes 2097152
  134.5 2.3 %copy.20 = f32[2048,128]{1,0:T(8,128)} copy(f32[2048,128]{1,0:T(8,128)} %get-tuple-element.7) | data formatting | bytes 2097152
Async XLA Ops:
  2.0 14.4 %all-to-all-start = ((s32[32,1,2]{2,1,0:T(1,128)}), s32[32,1,2]{2,1,0:T(1,128)S(1)}, u32[]{:S(2)}, u32[]{:S(2)}) async-start(s32[32,1,2]{2,1,0:T(1,128)} %bitcast.1), calls=%async_computation | async-start | bytes 32768 | tf_op jit(solution)/shard_map/all_to_all | solution.py:219
